TPU v7x, 32 devices: a whole 2x2x4 slice. The times are simulated.
32 devices in a mesh: groups: 2 (over y), dp: 16 (over z, x, core).
Axes of the slice: x: 2, y: 2, z: 4, core: 2. Of those that a mesh axis runs over, the one named last changes fastest.
Arguments:
- query_grads: bfloat16 [128, 8192], P('dp'), may hold values from -6 to 6
- train_factors: bfloat16 [32, 128, 512], P(('groups', 'dp')), parts along dimension 0, may hold values from -6 to 6
- lengths: int32 [32], P(('groups', 'dp')), parts along dimension 0, may hold values from 1 to 128, as said below
- owner: int32 [32], P('groups'), parts along dimension 0, may hold values from 0 to 15, each once
- basis_in: bfloat16 [8, 32, 32], replicated, may hold values from -1 to 1
- basis_out: bfloat16 [8, 32, 32], replicated, may hold values from -1 to 1
- eigenvalues: float32 [8, 32, 32], replicated, may hold values from 0.01 to 10
Outputs:
- scores: float32 [32, 128], P(('groups', 'dp')), parts along dimension 0
There are 2 independent parts, one for each index of `groups`. A program takes and returns all parts, laid end to end along the dimension named above; an argument that names none is the same for every part. Nothing has to cross between parts.
Inputs may be any that keep to these rules, and one draw needn't show every extreme that they name: `lengths`: every training sequence has at least one live token; in every draw some sequence is fully live. owner is a permutation of the training sequences.
All inputs are finite; a program needn't handle non-finite values.
Results may differ from a plain program's by a relative error of at most 0.0042.
Values may be sent and summed in bfloat16 or wider, within the bound.
A program may use at most 64 MiB of HBM per device.

v0:
```python
import math

import jax
import jax.numpy as jnp
from jax import lax
from jax.sharding import PartitionSpec as P


def from_behind(value, axis, steps):
    count = lax.axis_size(axis)
    pairs = [(source, (source + steps) % count) for source in range(count)]
    return lax.ppermute(value, axis, pairs)


def precondition(query_grads, basis_in, basis_out, eigenvalues):
    layers, rank = (eigenvalues.shape[0], eigenvalues.shape[1])
    grads = query_grads.reshape(query_grads.shape[0], layers, rank, rank).astype(jnp.float32)
    half = jnp.einsum("qlij,ljk->qlik", grads, basis_in.astype(jnp.float32)).astype(jnp.bfloat16)
    rotated = jnp.einsum("lio,qlik->qlok", basis_out.astype(jnp.float32), half.astype(jnp.float32))
    damp = 0.1 * jnp.mean(eigenvalues, axis=(1, 2), keepdims=True)
    scaled = rotated / (eigenvalues + damp)[None]
    return scaled.astype(jnp.bfloat16).reshape(query_grads.shape[0], layers * rank * rank)


def block_basis(basis_in, basis_out):
    layers, rank = (basis_in.shape[0], basis_in.shape[1])
    width = 2 * layers * rank
    table = jnp.zeros((width, width), jnp.bfloat16)
    for layer in range(layers):
        low = layer * rank
        table = table.at[low : low + rank, low : low + rank].set(basis_in[layer])
        high = (layers + layer) * rank
        table = table.at[high : high + rank, high : high + rank].set(basis_out[layer])
    return table


def gram_of(factors, lens, table, layers, rank):
    seqs, tokens = (factors.shape[0], factors.shape[1])
    rows = factors.reshape(seqs * tokens, factors.shape[2])
    rotated = jnp.dot(rows, table, preferred_element_type=jnp.float32).astype(jnp.bfloat16)
    rotated = rotated.reshape(seqs, tokens, 2, layers, rank).astype(jnp.float32)
    positions = lax.broadcasted_iota(jnp.int32, (seqs, tokens), 1)
    mask = (positions < lens[:, None]).astype(jnp.float32)
    outgrads = rotated[:, :, 1] * mask[:, :, None, None]
    gram = jnp.einsum("stlo,stlk->slok", outgrads, rotated[:, :, 0])
    return gram.reshape(seqs, layers * rank * rank)


def score_of(gram, precond, scale):
    return jnp.dot(gram, precond.astype(jnp.float32).T, precision=lax.Precision.HIGHEST) * scale


def route_rows(scores, owner):
    ordered = jnp.take(scores, owner, axis=0)
    return lax.all_to_all(ordered, "dp", split_axis=0, concat_axis=1, tiled=True)


def local(query_grads, train_factors, lengths, owner, basis_in, basis_out, eigenvalues):
    layers, rank = (eigenvalues.shape[0], eigenvalues.shape[1])
    ndev = lax.axis_size("dp")
    index = lax.axis_index("dp")
    seq_dev, tokens = (train_factors.shape[0], train_factors.shape[1])
    q_dev = query_grads.shape[0]
    seqs = owner.shape[0]
    scale = 1.0 / (rank * math.sqrt(tokens))
    precond = precondition(query_grads, basis_in, basis_out, eigenvalues)
    table = block_basis(basis_in, basis_out)
    own_gram = gram_of(train_factors, lengths, table, layers, rank)

    def turn_grams(step, carry):
        grams, scores = carry
        source = (index - step) % ndev
        piece = score_of(grams, precond, scale)
        scores = lax.dynamic_update_slice_in_dim(scores, piece, source * seq_dev, 0)
        grams = from_behind(grams, "dp", 1)
        return (grams, scores)

    start = jnp.zeros((seqs, q_dev), jnp.float32)
    grams, scores = lax.fori_loop(0, ndev - 1, turn_grams, (own_gram, start))
    source = (index - (ndev - 1)) % ndev
    scores = lax.dynamic_update_slice_in_dim(
        scores, score_of(grams, precond, scale), source * seq_dev, 0
    )
    return route_rows(scores, owner)


def solution(mesh):
    return jax.shard_map(
        local,
        mesh=mesh,
        in_specs=(
            P("dp", None),
            P(("groups", "dp"), None, None),
            P(("groups", "dp")),
            P("groups"),
            P(),
            P(),
            P(),
        ),
        out_specs=P(("groups", "dp"), None),
        check_vma=False,
    )
```

profile of v0, /device:TPU:0, one launch (start us, length us, event | category | flops | bytes accessed | tf_op | source)
XLA Modules:
  0.0 121.7 jit_solution(2784687971887223092)
XLA Ops:
  0.7 0.9 slice_bitcast_fusion.5
  2.8 0.8 scatter.56
  3.6 0.8 scatter.59
  8.4 0.8 scatter.70
  9.9 0.8 scatter.74
  13.5 0.8 copy-done.2
  16.3 1.1 fusion.4
  18.2 91.7 %while.33 = (s32[]{:T(128)}, f32[1,8192]{1,0:T(1,128)S(1)}, f32[16,8]{1,0:T(8,128)S(1)}, bf16[8,8192]{1,0:T(8,128)(2,1)S(1)}, s32[]{:T(128)}, /*index=5*/s32[]{:T(128)}, s32[]{:T(128)}, s32[]{:T(128)}, s32[]{:T(128)}) while((s32[]{:T(128)}, f32[1,8192]{1,0:T(1,128)S(1)}, f32[16,8]{1,0:T(8,128)S(1)}, bf16[8,8192]{1,0:T(8,128)(2,1)S(1)}, ...), condition=%wide.region_2.0_spmd, body=%wide.region_1.0_spmd.sunk | while | flops 786457 | bytes 360836 | solution.py:79
  19.1 6.2 %collective-permute-done = f32[1,8192]{1,0:T(1,128)S(1)} collective-permute-done((f32[1,8192]{1,0:T(1,128)S(1)}, f32[1,8192]{1,0:T(1,128)S(1)}, u32[]{:S(2)}, u32[]{:S(2)}) %collective-permute-start) | collective-permute-done | bytes 32800 | tf_op jit(solution)/shard_map/while/body/eval_jaxpr/ppermute | solution.py:12
  25.7 5.6 %collective-permute-done = f32[1,8192]{1,0:T(1,128)S(1)} collective-permute-done((f32[1,8192]{1,0:T(1,128)S(1)}, f32[1,8192]{1,0:T(1,128)S(1)}, u32[]{:S(2)}, u32[]{:S(2)}) %collective-permute-start) | collective-permute-done | bytes 32800 | tf_op jit(solution)/shard_map/while/body/eval_jaxpr/ppermute | solution.py:12
  31.7 5.6 %collective-permute-done = f32[1,8192]{1,0:T(1,128)S(1)} collective-permute-done((f32[1,8192]{1,0:T(1,128)S(1)}, f32[1,8192]{1,0:T(1,128)S(1)}, u32[]{:S(2)}, u32[]{:S(2)}) %collective-permute-start) | collective-permute-done | bytes 32800 | tf_op jit(solution)/shard_map/while/body/eval_jaxpr/ppermute | solution.py:12
  37.8 5.6 %collective-permute-done = f32[1,8192]{1,0:T(1,128)S(1)} collective-permute-done((f32[1,8192]{1,0:T(1,128)S(1)}, f32[1,8192]{1,0:T(1,128)S(1)}, u32[]{:S(2)}, u32[]{:S(2)}) %collective-permute-start) | collective-permute-done | bytes 32800 | tf_op jit(solution)/shard_map/while/body/eval_jaxpr/ppermute | solution.py:12
  43.8 5.6 %collective-permute-done = f32[1,8192]{1,0:T(1,128)S(1)} collective-permute-done((f32[1,8192]{1,0:T(1,128)S(1)}, f32[1,8192]{1,0:T(1,128)S(1)}, u32[]{:S(2)}, u32[]{:S(2)}) %collective-permute-start) | collective-permute-done | bytes 32800 | tf_op jit(solution)/shard_map/while/body/eval_jaxpr/ppermute | solution.py:12
  49.8 5.6 %collective-permute-done = f32[1,8192]{1,0:T(1,128)S(1)} collective-permute-done((f32[1,8192]{1,0:T(1,128)S(1)}, f32[1,8192]{1,0:T(1,128)S(1)}, u32[]{:S(2)}, u32[]{:S(2)}) %collective-permute-start) | collective-permute-done | bytes 32800 | tf_op jit(solution)/shard_map/while/body/eval_jaxpr/ppermute | solution.py:12
  55.9 5.6 %collective-permute-done = f32[1,8192]{1,0:T(1,128)S(1)} collective-permute-done((f32[1,8192]{1,0:T(1,128)S(1)}, f32[1,8192]{1,0:T(1,128)S(1)}, u32[]{:S(2)}, u32[]{:S(2)}) %collective-permute-start) | collective-permute-done | bytes 32800 | tf_op jit(solution)/shard_map/while/body/eval_jaxpr/ppermute | solution.py:12
  61.9 5.6 %collective-permute-done = f32[1,8192]{1,0:T(1,128)S(1)} collective-permute-done((f32[1,8192]{1,0:T(1,128)S(1)}, f32[1,8192]{1,0:T(1,128)S(1)}, u32[]{:S(2)}, u32[]{:S(2)}) %collective-permute-start) | collective-permute-done | bytes 32800 | tf_op jit(solution)/shard_map/while/body/eval_jaxpr/ppermute | solution.py:12
  68.0 5.6 %collective-permute-done = f32[1,8192]{1,0:T(1,128)S(1)} collective-permute-done((f32[1,8192]{1,0:T(1,128)S(1)}, f32[1,8192]{1,0:T(1,128)S(1)}, u32[]{:S(2)}, u32[]{:S(2)}) %collective-permute-start) | collective-permute-done | bytes 32800 | tf_op jit(solution)/shard_map/while/body/eval_jaxpr/ppermute | solution.py:12
  74.0 5.6 %collective-permute-done = f32[1,8192]{1,0:T(1,128)S(1)} collective-permute-done((f32[1,8192]{1,0:T(1,128)S(1)}, f32[1,8192]{1,0:T(1,128)S(1)}, u32[]{:S(2)}, u32[]{:S(2)}) %collective-permute-start) | collective-permute-done | bytes 32800 | tf_op jit(solution)/shard_map/while/body/eval_jaxpr/ppermute | solution.py:12
  80.0 5.6 %collective-permute-done = f32[1,8192]{1,0:T(1,128)S(1)} collective-permute-done((f32[1,8192]{1,0:T(1,128)S(1)}, f32[1,8192]{1,0:T(1,128)S(1)}, u32[]{:S(2)}, u32[]{:S(2)}) %collective-permute-start) | collective-permute-done | bytes 32800 | tf_op jit(solution)/shard_map/while/body/eval_jaxpr/ppermute | solution.py:12
  86.1 5.6 %collective-permute-done = f32[1,8192]{1,0:T(1,128)S(1)} collective-permute-done((f32[1,8192]{1,0:T(1,128)S(1)}, f32[1,8192]{1,0:T(1,128)S(1)}, u32[]{:S(2)}, u32[]{:S(2)}) %collective-permute-start) | collective-permute-done | bytes 32800 | tf_op jit(solution)/shard_map/while/body/eval_jaxpr/ppermute | solution.py:12
  92.1 5.6 %collective-permute-done = f32[1,8192]{1,0:T(1,128)S(1)} collective-permute-done((f32[1,8192]{1,0:T(1,128)S(1)}, f32[1,8192]{1,0:T(1,128)S(1)}, u32[]{:S(2)}, u32[]{:S(2)}) %collective-permute-start) | collective-permute-done | bytes 32800 | tf_op jit(solution)/shard_map/while/body/eval_jaxpr/ppermute | solution.py:12
  98.2 5.6 %collective-permute-done = f32[1,8192]{1,0:T(1,128)S(1)} collective-permute-done((f32[1,8192]{1,0:T(1,128)S(1)}, f32[1,8192]{1,0:T(1,128)S(1)}, u32[]{:S(2)}, u32[]{:S(2)}) %collective-permute-start) | collective-permute-done | bytes 32800 | tf_op jit(solution)/shard_map/while/body/eval_jaxpr/ppermute | solution.py:12
  104.2 5.6 %collective-permute-done = f32[1,8192]{1,0:T(1,128)S(1)} collective-permute-done((f32[1,8192]{1,0:T(1,128)S(1)}, f32[1,8192]{1,0:T(1,128)S(1)}, u32[]{:S(2)}, u32[]{:S(2)}) %collective-permute-start) | collective-permute-done | bytes 32800 | tf_op jit(solution)/shard_map/while/body/eval_jaxpr/ppermute | solution.py:12
  111.0 9.0 %all_to_all.13 = f32[16,1,8]{2,1,0:T(1,128)S(1)} all-to-all(f32[16,1,8]{2,1,0:T(1,128)S(1)} %copy.20), channel_id=1, replica_groups=mesh['groups'=2,'dp'=16] {'dp'}, dimensions={0} | all-to-all | bytes 1024 | tf_op jit(solution)/shard_map/all_to_all | solution.py:55
  (108 shorter events, 21.0 us)
Async XLA Ops:
  0.0 12.8 %copy-start = (bf16[1,128,512]{2,1,0:T(8,128)(2,1)S(1)}, bf16[1,128,512]{2,1,0:T(8,128)(2,1)}, u32[]{:S(2)}) copy-start(bf16[1,128,512]{2,1,0:T(8,128)(2,1)} %param.42) | copy-start | bytes 393220
  0.0 0.7 copy-start.5
  0.7 0.9 copy-start.4
  13.3 0.9 copy-start.2
  14.3 0.9 copy-start.1
  15.4 0.8 copy-start.3
  18.2 7.1 %collective-permute-start = (f32[1,8192]{1,0:T(1,128)S(1)}, f32[1,8192]{1,0:T(1,128)S(1)}, u32[]{:S(2)}, u32[]{:S(2)}) collective-permute-start(f32[1,8192]{1,0:T(1,128)S(1)} %copy.48), channel_id=1, source_target_pairs={{0,1},{1,2},{2,3},{3,4},{4,5},{5,6},{6,7},{7,8},{8,9},{9,10},{10,1... | collective-permute-start | bytes 98312 | tf_op jit(solution)/shard_map/while/body/eval_jaxpr/ppermute | solution.py:12
  25.3 6.0 %collective-permute-start = (f32[1,8192]{1,0:T(1,128)S(1)}, f32[1,8192]{1,0:T(1,128)S(1)}, u32[]{:S(2)}, u32[]{:S(2)}) collective-permute-start(f32[1,8192]{1,0:T(1,128)S(1)} %copy.48), channel_id=1, source_target_pairs={{0,1},{1,2},{2,3},{3,4},{4,5},{5,6},{6,7},{7,8},{8,9},{9,10},{10,1... | collective-permute-start | bytes 98312 | tf_op jit(solution)/shard_map/while/body/eval_jaxpr/ppermute | solution.py:12
  31.3 6.0 %collective-permute-start = (f32[1,8192]{1,0:T(1,128)S(1)}, f32[1,8192]{1,0:T(1,128)S(1)}, u32[]{:S(2)}, u32[]{:S(2)}) collective-permute-start(f32[1,8192]{1,0:T(1,128)S(1)} %copy.48), channel_id=1, source_target_pairs={{0,1},{1,2},{2,3},{3,4},{4,5},{5,6},{6,7},{7,8},{8,9},{9,10},{10,1... | collective-permute-start | bytes 98312 | tf_op jit(solution)/shard_map/while/body/eval_jaxpr/ppermute | solution.py:12
  37.3 6.0 %collective-permute-start = (f32[1,8192]{1,0:T(1,128)S(1)}, f32[1,8192]{1,0:T(1,128)S(1)}, u32[]{:S(2)}, u32[]{:S(2)}) collective-permute-start(f32[1,8192]{1,0:T(1,128)S(1)} %copy.48), channel_id=1, source_target_pairs={{0,1},{1,2},{2,3},{3,4},{4,5},{5,6},{6,7},{7,8},{8,9},{9,10},{10,1... | collective-permute-start | bytes 98312 | tf_op jit(solution)/shard_map/while/body/eval_jaxpr/ppermute | solution.py:12
  43.4 6.0 %collective-permute-start = (f32[1,8192]{1,0:T(1,128)S(1)}, f32[1,8192]{1,0:T(1,128)S(1)}, u32[]{:S(2)}, u32[]{:S(2)}) collective-permute-start(f32[1,8192]{1,0:T(1,128)S(1)} %copy.48), channel_id=1, source_target_pairs={{0,1},{1,2},{2,3},{3,4},{4,5},{5,6},{6,7},{7,8},{8,9},{9,10},{10,1... | collective-permute-start | bytes 98312 | tf_op jit(solution)/shard_map/while/body/eval_jaxpr/ppermute | solution.py:12
  49.4 6.0 %collective-permute-start = (f32[1,8192]{1,0:T(1,128)S(1)}, f32[1,8192]{1,0:T(1,128)S(1)}, u32[]{:S(2)}, u32[]{:S(2)}) collective-permute-start(f32[1,8192]{1,0:T(1,128)S(1)} %copy.48), channel_id=1, source_target_pairs={{0,1},{1,2},{2,3},{3,4},{4,5},{5,6},{6,7},{7,8},{8,9},{9,10},{10,1... | collective-permute-start | bytes 98312 | tf_op jit(solution)/shard_map/while/body/eval_jaxpr/ppermute | solution.py:12
  55.5 6.0 %collective-permute-start = (f32[1,8192]{1,0:T(1,128)S(1)}, f32[1,8192]{1,0:T(1,128)S(1)}, u32[]{:S(2)}, u32[]{:S(2)}) collective-permute-start(f32[1,8192]{1,0:T(1,128)S(1)} %copy.48), channel_id=1, source_target_pairs={{0,1},{1,2},{2,3},{3,4},{4,5},{5,6},{6,7},{7,8},{8,9},{9,10},{10,1... | collective-permute-start | bytes 98312 | tf_op jit(solution)/shard_map/while/body/eval_jaxpr/ppermute | solution.py:12
  61.5 6.0 %collective-permute-start = (f32[1,8192]{1,0:T(1,128)S(1)}, f32[1,8192]{1,0:T(1,128)S(1)}, u32[]{:S(2)}, u32[]{:S(2)}) collective-permute-start(f32[1,8192]{1,0:T(1,128)S(1)} %copy.48), channel_id=1, source_target_pairs={{0,1},{1,2},{2,3},{3,4},{4,5},{5,6},{6,7},{7,8},{8,9},{9,10},{10,1... | collective-permute-start | bytes 98312 | tf_op jit(solution)/shard_map/while/body/eval_jaxpr/ppermute | solution.py:12
  67.6 6.0 %collective-permute-start = (f32[1,8192]{1,0:T(1,128)S(1)}, f32[1,8192]{1,0:T(1,128)S(1)}, u32[]{:S(2)}, u32[]{:S(2)}) collective-permute-start(f32[1,8192]{1,0:T(1,128)S(1)} %copy.48), channel_id=1, source_target_pairs={{0,1},{1,2},{2,3},{3,4},{4,5},{5,6},{6,7},{7,8},{8,9},{9,10},{10,1... | collective-permute-start | bytes 98312 | tf_op jit(solution)/shard_map/while/body/eval_jaxpr/ppermute | solution.py:12
  73.6 6.0 %collective-permute-start = (f32[1,8192]{1,0:T(1,128)S(1)}, f32[1,8192]{1,0:T(1,128)S(1)}, u32[]{:S(2)}, u32[]{:S(2)}) collective-permute-start(f32[1,8192]{1,0:T(1,128)S(1)} %copy.48), channel_id=1, source_target_pairs={{0,1},{1,2},{2,3},{3,4},{4,5},{5,6},{6,7},{7,8},{8,9},{9,10},{10,1... | collective-permute-start | bytes 98312 | tf_op jit(solution)/shard_map/while/body/eval_jaxpr/ppermute | solution.py:12
  79.6 6.0 %collective-permute-start = (f32[1,8192]{1,0:T(1,128)S(1)}, f32[1,8192]{1,0:T(1,128)S(1)}, u32[]{:S(2)}, u32[]{:S(2)}) collective-permute-start(f32[1,8192]{1,0:T(1,128)S(1)} %copy.48), channel_id=1, source_target_pairs={{0,1},{1,2},{2,3},{3,4},{4,5},{5,6},{6,7},{7,8},{8,9},{9,10},{10,1... | collective-permute-start | bytes 98312 | tf_op jit(solution)/shard_map/while/body/eval_jaxpr/ppermute | solution.py:12
  85.7 6.0 %collective-permute-start = (f32[1,8192]{1,0:T(1,128)S(1)}, f32[1,8192]{1,0:T(1,128)S(1)}, u32[]{:S(2)}, u32[]{:S(2)}) collective-permute-start(f32[1,8192]{1,0:T(1,128)S(1)} %copy.48), channel_id=1, source_target_pairs={{0,1},{1,2},{2,3},{3,4},{4,5},{5,6},{6,7},{7,8},{8,9},{9,10},{10,1... | collective-permute-start | bytes 98312 | tf_op jit(solution)/shard_map/while/body/eval_jaxpr/ppermute | solution.py:12
  91.7 6.0 %collective-permute-start = (f32[1,8192]{1,0:T(1,128)S(1)}, f32[1,8192]{1,0:T(1,128)S(1)}, u32[]{:S(2)}, u32[]{:S(2)}) collective-permute-start(f32[1,8192]{1,0:T(1,128)S(1)} %copy.48), channel_id=1, source_target_pairs={{0,1},{1,2},{2,3},{3,4},{4,5},{5,6},{6,7},{7,8},{8,9},{9,10},{10,1... | collective-permute-start | bytes 98312 | tf_op jit(solution)/shard_map/while/body/eval_jaxpr/ppermute | solution.py:12
  97.8 6.0 %collective-permute-start = (f32[1,8192]{1,0:T(1,128)S(1)}, f32[1,8192]{1,0:T(1,128)S(1)}, u32[]{:S(2)}, u32[]{:S(2)}) collective-permute-start(f32[1,8192]{1,0:T(1,128)S(1)} %copy.48), channel_id=1, source_target_pairs={{0,1},{1,2},{2,3},{3,4},{4,5},{5,6},{6,7},{7,8},{8,9},{9,10},{10,1... | collective-permute-start | bytes 98312 | tf_op jit(solution)/shard_map/while/body/eval_jaxpr/ppermute | solution.py:12
  103.8 6.0 %collective-permute-start = (f32[1,8192]{1,0:T(1,128)S(1)}, f32[1,8192]{1,0:T(1,128)S(1)}, u32[]{:S(2)}, u32[]{:S(2)}) collective-permute-start(f32[1,8192]{1,0:T(1,128)S(1)} %copy.48), channel_id=1, source_target_pairs={{0,1},{1,2},{2,3},{3,4},{4,5},{5,6},{6,7},{7,8},{8,9},{9,10},{10,1... | collective-permute-start | bytes 98312 | tf_op jit(solution)/shard_map/while/body/eval_jaxpr/ppermute | solution.py:12
where the time goes:
time: 122 us
  waiting for transfers between devices  84.9 us (70%)
  local copies, waits for them, and re-layouts  17.8 us (15%)
  blocking collectives  8.97 us (7%)
  matrix products  7.49 us (6%)
    ppermute x15, waiting for transfers between devices, from_behind(): return lax.ppermute(value, axis, pairs)  84.9 us
    all_to_all x1, blocking collectives, route_rows(): lax.all_to_all(ordered, 'dp', split_axis=0, concat_axis=1, tiled=True)  8.97 us
    dot_general x16, matrix products, score_of(): jnp.dot(gram, precond.astype(jnp.float32).T, precision=lax.Precision.HIGH...  5.93 us
    scatter x8, local copies, waits for them, and re-layouts, block_basis(): table = table.at[high:high + rank, high:high + rank].set(basis_out[layer])  5.29 us
    scatter x8, local copies, waits for them, and re-layouts, block_basis(): table = table.at[low:low + rank, low:low + rank].set(basis_in[layer])  5.17 us
    unnamed x12, local copies, waits for them, and re-layouts  2.75 us
  transfers between devices with their start and end apart: 15, of which 15 were waited for; matrix products, arithmetic and copies ran while one was open for 5% of the time, Pallas kernels for 0%

commit v1 on v0

v1 whole, which is shorter than its diff:
```python
import functools
import math

import jax
import jax.numpy as jnp
from jax import lax
from jax.experimental import pallas as pl
from jax.experimental.pallas import tpu as pltpu
from jax.sharding import PartitionSpec as P

LANES = 128
SUB = 8
NT = (((1,), (1,)), ((), ()))


def nt_dot(a, b, **kw):
    return lax.dot_general(a, b, NT, preferred_element_type=jnp.float32, **kw)


def nn_dot(a, b, **kw):
    return jnp.dot(a, b, preferred_element_type=jnp.float32, **kw)


def iota(shape, dim):
    return lax.broadcasted_iota(jnp.int32, shape, dim)


def each(count, body):
    if count <= 16:
        for step in range(count):
            body(step)
    else:
        lax.fori_loop(0, count, lambda step, c: (body(step), c)[1], 0)


def kernel(n, parts, layers, rank, tokens, q_dev,
           len_ref, own_ref, grads_hbm, fact_hbm, bin_hbm, bout_hbm, eig_hbm,
           out_ref,
           fact, b_in, b_out, eig, bo32, gbuf, hsend, hbuf, score, ssend, sbuf,
           load_sem, gself_sem, gsend_sem, grecv_sem,
           hsend_sem, hrecv_sem, ssend_sem, srecv_sem):
    me = lax.axis_index("dp")
    group = me // parts
    part = me % parts
    width = layers * rank
    feats = layers * rank * rank
    share = feats // parts
    chunks = share // LANES
    per = LANES // rank

    loads = [
        pltpu.make_async_copy(src, dst, load_sem.at[i])
        for i, (src, dst) in enumerate(
            [(bin_hbm, b_in), (bout_hbm, b_out), (eig_hbm, eig), (fact_hbm, fact)]
        )
    ]
    for load in loads:
        load.start()
    own_grads = pltpu.make_async_copy(
        grads_hbm.at[:, pl.ds(pl.multiple_of(part * share, share), share)],
        gbuf.at[part], gself_sem)
    own_grads.start()

    barrier = pltpu.get_barrier_semaphore()

    def greet(step):
        peer = (me + step + 1) % n
        pl.semaphore_signal(barrier, inc=1, device_id={"dp": peer},
                            device_id_type=pl.DeviceIdType.MESH)

    each(n - 1, greet)
    pl.semaphore_wait(barrier, n - 1)

    def send_grads(step):
        other = (part + step + 1) % parts
        pltpu.make_async_remote_copy(
            grads_hbm.at[:, pl.ds(pl.multiple_of(other * share, share), share)],
            gbuf.at[part], gsend_sem, grecv_sem,
            device_id={"dp": group * parts + other},
            device_id_type=pl.DeviceIdType.MESH).start()

    each(parts - 1, send_grads)

    for load in loads[:3]:
        load.wait()
    bi = b_in[...].reshape(width, rank)
    bo = b_out[...].reshape(width, rank)
    spread = (iota((rank, width), 0) == iota((rank, width), 1) % rank).astype(jnp.bfloat16)
    spread_t = (iota((width, rank), 0) % rank == iota((width, rank), 1)).astype(jnp.bfloat16)
    lane_layer = iota((width, width), 1) // rank
    same = iota((width, width), 0) // rank == lane_layer
    diag_in32 = jnp.where(same, nn_dot(bi, spread), 0.0)
    diag_in = diag_in32.astype(jnp.bfloat16)
    diag_out_t = jnp.where(same, nt_dot(spread_t, bo), 0.0).astype(jnp.bfloat16)
    rows_in = jnp.sum(diag_in32.reshape(layers, rank, width), axis=0)
    rows_in = jnp.concatenate([rows_in] * per, axis=0).astype(jnp.bfloat16)
    bo32[...] = bo.astype(jnp.float32)
    shuffled = jnp.concatenate(
        [bo32[pl.ds(low, width // per, stride=per), :] for low in range(per)], axis=0
    ).astype(jnp.bfloat16)
    in_order = (iota((width, width), 0) % (width // per)) // (rank // per) == lane_layer
    diag_out = jnp.where(in_order, nn_dot(shuffled, spread), 0.0).astype(jnp.bfloat16)
    values = eig[...]
    damp = 0.1 * (jnp.sum(values, axis=(1, 2), keepdims=True) * (1.0 / (rank * rank)))
    weight = (1.0 / (values + damp)).reshape(width, rank)
    weight = nn_dot(weight, spread.astype(jnp.float32), precision=lax.Precision.HIGHEST)
    weight = jnp.where(same, weight, 0.0)

    loads[3].wait()
    rot_in = nn_dot(fact[0, :, :width], diag_in).astype(jnp.bfloat16)
    rot_out = nt_dot(diag_out_t, fact[0, :, width:])
    live = iota((width, tokens), 1) < len_ref[0]
    rot_out = jnp.where(live, rot_out, 0.0).astype(jnp.bfloat16)
    gram = nn_dot(rot_out, rot_in)
    scaled = (gram * weight).astype(jnp.bfloat16)
    back = nt_dot(scaled, rows_in).astype(jnp.bfloat16)
    back = nn_dot(diag_out, back)
    rows = width // per
    slot = iota((rows, LANES), 1) // rank
    total = jnp.zeros((rows, LANES), jnp.float32)
    for low in range(per):
        total = jnp.where(slot == low, back[low * rows:(low + 1) * rows], total)
    hsend[...] = total

    def part_rows(which):
        return pl.ds(pl.multiple_of(which * chunks, chunks), chunks)

    def send_rows(step):
        peer = (me + step + 1) % n
        pltpu.make_async_remote_copy(
            hsend.at[part_rows(peer % parts)], hbuf.at[part_rows(me)],
            hsend_sem, hrecv_sem, device_id={"dp": peer},
            device_id_type=pl.DeviceIdType.MESH).start()

    each(n - 1, send_rows)
    hbuf[part_rows(me), :] = hsend[part_rows(part), :]

    own_grads.wait()
    some = gbuf.at[pl.ds(0, parts - 1)]
    pltpu.make_async_copy(some, some, grecv_sem).wait()
    grads = gbuf[...].astype(jnp.float32).reshape(parts * q_dev, share).astype(jnp.bfloat16)
    grads = jnp.concatenate([grads] * (LANES // (parts * q_dev)), axis=0)
    others = hbuf.at[pl.ds(0, (n - 1) * chunks)]
    pltpu.make_async_copy(others, others, hrecv_sem).wait()
    sums = jnp.concatenate(
        [hbuf[pl.ds(c, n, stride=chunks), :].astype(jnp.bfloat16) for c in range(chunks)], axis=1)
    score[...] = nt_dot(sums, grads)

    def order(step):
        ssend[step] = score[pl.ds(own_ref[step], 1), :]

    each(n, order)

    def send_score(step):
        peer = (me + step + 1) % n
        pltpu.make_async_remote_copy(
            ssend.at[peer], sbuf.at[me], ssend_sem, srecv_sem, device_id={"dp": peer},
            device_id_type=pl.DeviceIdType.MESH).start()

    each(n - 1, send_score)
    sbuf[me] = ssend[me]
    rest = sbuf.at[pl.ds(0, n - 1)]
    pltpu.make_async_copy(rest, rest, srecv_sem).wait()

    scale = 1.0 / (rank * math.sqrt(tokens))
    span = parts * q_dev
    lane = iota((1, LANES), 1) // span
    per_block = LANES // span
    for block in range(n // parts // per_block):
        row = jnp.zeros((1, LANES), jnp.float32)
        for at in range(per_block):
            low = (block * per_block + at) * parts
            row = jnp.where(lane == at, jnp.sum(sbuf[low:low + parts], axis=0), row)
        out_ref[:, block * LANES:(block + 1) * LANES] = row * scale

    pltpu.make_async_copy(some, some, gsend_sem).wait()
    pltpu.make_async_copy(others, others, hsend_sem).wait()
    pltpu.make_async_copy(rest, rest, ssend_sem).wait()


def local(query_grads, train_factors, lengths, owner, basis_in, basis_out, eigenvalues):
    layers, rank = (eigenvalues.shape[0], eigenvalues.shape[1])
    n = lax.axis_size("dp")
    seqs, tokens, cols = train_factors.shape
    q_dev, feats = query_grads.shape
    parts = feats // (SUB * LANES)
    share = feats // parts
    width = layers * rank
    chunks = share // LANES
    hbm = pl.BlockSpec(memory_space=pl.ANY)
    smem = pl.BlockSpec(memory_space=pltpu.SMEM)
    dma = pltpu.SemaphoreType.DMA
    return pl.pallas_call(
        functools.partial(kernel, n, parts, layers, rank, tokens, q_dev),
        out_shape=jax.ShapeDtypeStruct((1, n * q_dev), jnp.float32),
        in_specs=[smem, smem, hbm, hbm, hbm, hbm, hbm],
        out_specs=pl.BlockSpec(memory_space=pltpu.VMEM),
        scratch_shapes=[
            pltpu.VMEM((seqs, tokens, cols), jnp.bfloat16),
            pltpu.VMEM((layers, rank, rank), jnp.bfloat16),
            pltpu.VMEM((layers, rank, rank), jnp.bfloat16),
            pltpu.VMEM((layers, rank, rank), jnp.float32),
            pltpu.VMEM((width, rank), jnp.float32),
            pltpu.VMEM((parts, q_dev, share), jnp.bfloat16),
            pltpu.VMEM((feats // LANES, LANES), jnp.float32),
            pltpu.VMEM((n * chunks, LANES), jnp.float32),
            pltpu.VMEM((n, LANES), jnp.float32),
            pltpu.VMEM((n, 1, LANES), jnp.float32),
            pltpu.VMEM((n, 1, LANES), jnp.float32),
            dma((4,)), dma, dma, dma, dma, dma, dma, dma,
        ],
        compiler_params=pltpu.CompilerParams(
            collective_id=0, has_side_effects=True, vmem_limit_bytes=32 * 1024 * 1024),
    )(lengths, owner, query_grads, train_factors, basis_in, basis_out, eigenvalues)


def solution(mesh):
    return jax.shard_map(
        local,
        mesh=mesh,
        in_specs=(
            P("dp", None),
            P(("groups", "dp"), None, None),
            P(("groups", "dp")),
            P("groups"),
            P(),
            P(),
            P(),
        ),
        out_specs=P(("groups", "dp"), None),
        check_vma=False,
    )
```

time: 122 us -> 23 us (0.19)
  waiting for transfers between devices: 84.9 us -> 0 us
  Pallas kernels: 0 us -> 17.1 us
  local copies, waits for them, and re-layouts: 17.8 us -> 4.9 us
  blocking collectives: 8.97 us -> 0 us
  matrix products: 7.49 us -> 0 us
    ppermute x15 -> x0, waiting for transfers between devices: 84.9 us -> none  [from_behind(): return lax.ppermute(value, axis, pairs)]
    pallas_call x0 -> x1, Pallas kernels: none -> 17.1 us  [local(): pl.pallas_call(functools.partial(kernel, n, parts, layers, rank, tokens,...]
    scatter x16 -> x0, local copies, waits for them, and re-layouts: 10.5 us -> none  [the longest x8 5.29 us: block_basis(): table = table.at[high:high + rank, high:high + rank].set(basis_out[layer])]
    all_to_all x1 -> x0, blocking collectives: 8.97 us -> none  [route_rows(): lax.all_to_all(ordered, 'dp', split_axis=0, concat_axis=1, tiled=True)]
    dot_general x19 -> x0, matrix products: 7.49 us -> none  [the longest x16 5.93 us: score_of(): jnp.dot(gram, precond.astype(jnp.float32).T, precision=lax.Precision.HIGH...]
    unnamed x12 -> x13, local copies, waits for them, and re-layouts: 2.75 us -> 4.9 us
  transfers between devices with their start and end apart: 15 -> 0, of which waited for: 15 -> 0; matrix products, arithmetic and copies ran while one was open for 5% -> 0% of each run, Pallas kernels for 0% -> 0%
where the time goes in v1:
time: 23 us; the launch traced here: 22.7 us
  Pallas kernels  17.1 us (74%)
  local copies, waits for them, and re-layouts  4.9 us (21%)
  between operations  0.7 us (3%)
    pallas_call x1, Pallas kernels, local(): pl.pallas_call(functools.partial(kernel, n, parts, layers, rank, tokens,...  17.1 us
    unnamed x13, local copies, waits for them, and re-layouts  4.9 us

profile of v1, /device:TPU:0, one launch (start us, length us, event | category | flops | bytes accessed | tf_op | source)
XLA Modules:
  0.0 22.7 jit_solution(7226216691107382742)
XLA Ops:
  0.0 0.0 copy-start.5
  0.7 0.0 copy-done.5
  0.7 0.0 copy-start
  0.7 0.9 %copy-done = bf16[8,8192]{1,0:T(8,128)(2,1)S(1)} copy-done((bf16[8,8192]{1,0:T(8,128)(2,1)S(1)}, bf16[8,8192]{1,0:T(8,128)(2,1)}, u32[]{:S(2)}) %copy-start) | copy-done | bytes 131096
  1.6 0.0 copy-start.1
  1.6 0.9 %copy-done.1 = bf16[1,128,512]{2,1,0:T(8,128)(2,1)S(1)} copy-done((bf16[1,128,512]{2,1,0:T(8,128)(2,1)S(1)}, bf16[1,128,512]{2,1,0:T(8,128)(2,1)}, u32[]{:S(2)}) %copy-start.1) | copy-done | bytes 131096
  2.5 0.0 copy-start.2
  2.5 0.9 %copy-done.2 = f32[8,32,32]{2,1,0:T(8,128)S(1)} copy-done((f32[8,32,32]{2,1,0:T(8,128)S(1)}, f32[8,32,32]{2,1,0:T(8,128)}, u32[]{:S(2)}) %copy-start.2) | copy-done | bytes 32792
  3.4 0.0 copy-start.3
  3.4 0.8 %copy-done.3 = bf16[8,32,32]{2,1,0:T(8,128)(2,1)S(1)} copy-done((bf16[8,32,32]{2,1,0:T(8,128)(2,1)S(1)}, bf16[8,32,32]{2,1,0:T(8,128)(2,1)}, u32[]{:S(2)}) %copy-start.3) | copy-done | bytes 16408
  4.2 0.0 copy-start.4
  4.2 0.8 %copy-done.4 = bf16[8,32,32]{2,1,0:T(8,128)(2,1)S(1)} copy-done((bf16[8,32,32]{2,1,0:T(8,128)(2,1)S(1)}, bf16[8,32,32]{2,1,0:T(8,128)(2,1)}, u32[]{:S(2)}) %copy-start.4) | copy-done | bytes 16408
  5.1 17.1 %shard_map.73 = f32[1,128]{1,0:T(1,128)S(1)} custom-call(s32[1]{0:T(128)S(6)} %copy.9.len_ref, s32[16]{0:T(128)S(1)} %copy-done.5, bf16[8,8192]{1,0:T(8,128)(2,1)S(1)} %copy-done, bf16[1,128,512]{2,1,0:T(8,128)(2,1)S(1)} %copy-done.1, bf16[8,32,32]{2,1,0:T(8,128)(2,1)S(1)} %copy-done.3, bf16[8,32,32]{2,1,0:T(8,128)(2,1)S(1)} %copy-done.4, ...), custom_call_target="tpu_custom_call" | custom-call | tf_op jit(solution)/shard_map/pallas_call | solution.py:193
  22.2 0.5 %copy.10 = f32[1,128]{1,0:T(1,128)} copy(f32[1,128]{1,0:T(1,128)S(1)} %shard_map.73) | data formatting | bytes 1024
Async XLA Ops:
  0.0 0.7 %copy-start.5 = (s32[16]{0:T(128)S(1)}, s32[16]{0:T(128)}, u32[]{:S(2)}) copy-start(s32[16]{0:T(128)} %own_ref.1) | copy-start | bytes 196
  0.7 0.9 %copy-start = (bf16[8,8192]{1,0:T(8,128)(2,1)S(1)}, bf16[8,8192]{1,0:T(8,128)(2,1)}, u32[]{:S(2)}) copy-start(bf16[8,8192]{1,0:T(8,128)(2,1)} %grads_hbm.1) | copy-start | bytes 393220
  1.6 0.9 %copy-start.1 = (bf16[1,128,512]{2,1,0:T(8,128)(2,1)S(1)}, bf16[1,128,512]{2,1,0:T(8,128)(2,1)}, u32[]{:S(2)}) copy-start(bf16[1,128,512]{2,1,0:T(8,128)(2,1)} %fact_hbm.1) | copy-start | bytes 393220
  2.5 0.9 %copy-start.2 = (f32[8,32,32]{2,1,0:T(8,128)S(1)}, f32[8,32,32]{2,1,0:T(8,128)}, u32[]{:S(2)}) copy-start(f32[8,32,32]{2,1,0:T(8,128)} %eig_hbm.1) | copy-start | bytes 98308
  3.4 0.8 %copy-start.3 = (bf16[8,32,32]{2,1,0:T(8,128)(2,1)S(1)}, bf16[8,32,32]{2,1,0:T(8,128)(2,1)}, u32[]{:S(2)}) copy-start(bf16[8,32,32]{2,1,0:T(8,128)(2,1)} %bin_hbm.1) | copy-start | bytes 49156
  4.2 0.8 %copy-start.4 = (bf16[8,32,32]{2,1,0:T(8,128)(2,1)S(1)}, bf16[8,32,32]{2,1,0:T(8,128)(2,1)}, u32[]{:S(2)}) copy-start(bf16[8,32,32]{2,1,0:T(8,128)(2,1)} %bout_hbm.1) | copy-start | bytes 49156

commit v2 on v1

--- a/solution.py
+++ b/solution.py
@@ -34,9 +34,9 @@
 
 
 def kernel(n, parts, layers, rank, tokens, q_dev,
-           len_ref, own_ref, grads_hbm, fact_hbm, bin_hbm, bout_hbm, eig_hbm,
+           len_hbm, own_hbm, grads_hbm, fact_hbm, bin_hbm, bout_hbm, eig_hbm,
            out_ref,
-           fact, b_in, b_out, eig, bo32, gbuf, hsend, hbuf, score, ssend, sbuf,
+           len_ref, own_ref, fact, b_in, b_out, eig, bo32, gbuf, hsend, hbuf, wide, score, ssend, sbuf,
            load_sem, gself_sem, gsend_sem, grecv_sem,
            hsend_sem, hrecv_sem, ssend_sem, srecv_sem):
     me = lax.axis_index("dp")
@@ -51,7 +51,8 @@
     loads = [
         pltpu.make_async_copy(src, dst, load_sem.at[i])
         for i, (src, dst) in enumerate(
-            [(bin_hbm, b_in), (bout_hbm, b_out), (eig_hbm, eig), (fact_hbm, fact)]
+            [(bin_hbm, b_in), (bout_hbm, b_out), (eig_hbm, eig), (fact_hbm, fact),
+             (len_hbm, len_ref), (own_hbm, own_ref)]
         )
     ]
     for load in loads:
@@ -106,7 +107,8 @@
     weight = nn_dot(weight, spread.astype(jnp.float32), precision=lax.Precision.HIGHEST)
     weight = jnp.where(same, weight, 0.0)
 
-    loads[3].wait()
+    for load in loads[3:]:
+        load.wait()
     rot_in = nn_dot(fact[0, :, :width], diag_in).astype(jnp.bfloat16)
     rot_out = nt_dot(diag_out_t, fact[0, :, width:])
     live = iota((width, tokens), 1) < len_ref[0]
@@ -120,30 +122,28 @@
     total = jnp.zeros((rows, LANES), jnp.float32)
     for low in range(per):
         total = jnp.where(slot == low, back[low * rows:(low + 1) * rows], total)
-    hsend[...] = total
-
-    def part_rows(which):
-        return pl.ds(pl.multiple_of(which * chunks, chunks), chunks)
+    hsend[...] = total.reshape(parts, chunks, LANES).astype(jnp.bfloat16)
 
     def send_rows(step):
         peer = (me + step + 1) % n
         pltpu.make_async_remote_copy(
-            hsend.at[part_rows(peer % parts)], hbuf.at[part_rows(me)],
+            hsend.at[peer % parts], hbuf.at[me],
             hsend_sem, hrecv_sem, device_id={"dp": peer},
             device_id_type=pl.DeviceIdType.MESH).start()
 
     each(n - 1, send_rows)
-    hbuf[part_rows(me), :] = hsend[part_rows(part), :]
+    hbuf[me] = hsend[part]
 
     own_grads.wait()
     some = gbuf.at[pl.ds(0, parts - 1)]
     pltpu.make_async_copy(some, some, grecv_sem).wait()
     grads = gbuf[...].astype(jnp.float32).reshape(parts * q_dev, share).astype(jnp.bfloat16)
     grads = jnp.concatenate([grads] * (LANES // (parts * q_dev)), axis=0)
-    others = hbuf.at[pl.ds(0, (n - 1) * chunks)]
+    others = hbuf.at[pl.ds(0, n - 1)]
     pltpu.make_async_copy(others, others, hrecv_sem).wait()
+    wide[...] = hbuf[...].astype(jnp.float32).reshape(n * chunks, LANES)
     sums = jnp.concatenate(
-        [hbuf[pl.ds(c, n, stride=chunks), :].astype(jnp.bfloat16) for c in range(chunks)], axis=1)
+        [wide[pl.ds(c, n, stride=chunks), :].astype(jnp.bfloat16) for c in range(chunks)], axis=1)
     score[...] = nt_dot(sums, grads)
 
     def order(step):
@@ -187,30 +187,32 @@
     share = feats // parts
     width = layers * rank
     chunks = share // LANES
-    hbm = pl.BlockSpec(memory_space=pl.ANY)
-    smem = pl.BlockSpec(memory_space=pltpu.SMEM)
+    hbm = pl.BlockSpec(memory_space=pltpu.HBM)
     dma = pltpu.SemaphoreType.DMA
     return pl.pallas_call(
         functools.partial(kernel, n, parts, layers, rank, tokens, q_dev),
         out_shape=jax.ShapeDtypeStruct((1, n * q_dev), jnp.float32),
-        in_specs=[smem, smem, hbm, hbm, hbm, hbm, hbm],
+        in_specs=[hbm] * 7,
         out_specs=pl.BlockSpec(memory_space=pltpu.VMEM),
         scratch_shapes=[
+            pltpu.SMEM(lengths.shape, jnp.int32),
+            pltpu.SMEM(owner.shape, jnp.int32),
             pltpu.VMEM((seqs, tokens, cols), jnp.bfloat16),
             pltpu.VMEM((layers, rank, rank), jnp.bfloat16),
             pltpu.VMEM((layers, rank, rank), jnp.bfloat16),
             pltpu.VMEM((layers, rank, rank), jnp.float32),
             pltpu.VMEM((width, rank), jnp.float32),
             pltpu.VMEM((parts, q_dev, share), jnp.bfloat16),
-            pltpu.VMEM((feats // LANES, LANES), jnp.float32),
+            pltpu.VMEM((parts, chunks, LANES), jnp.bfloat16),
+            pltpu.VMEM((n, chunks, LANES), jnp.bfloat16),
             pltpu.VMEM((n * chunks, LANES), jnp.float32),
             pltpu.VMEM((n, LANES), jnp.float32),
             pltpu.VMEM((n, 1, LANES), jnp.float32),
             pltpu.VMEM((n, 1, LANES), jnp.float32),
-            dma((4,)), dma, dma, dma, dma, dma, dma, dma,
+            dma((6,)), dma, dma, dma, dma, dma, dma, dma,
         ],
         compiler_params=pltpu.CompilerParams(
-            collective_id=0, has_side_effects=True, vmem_limit_bytes=32 * 1024 * 1024),
+            collective_id=0, has_side_effects=True),
     )(lengths, owner, query_grads, train_factors, basis_in, basis_out, eigenvalues)
 
 

time: 23 us -> 18.4 us (0.80)
  local copies, waits for them, and re-layouts: 4.9 us -> 1.19 us
  Pallas kernels: 17.1 us -> 16.4 us
    unnamed x13 -> x1, local copies, waits for them, and re-layouts: 4.9 us -> 1.19 us
    pallas_call x1, Pallas kernels: 17.1 us -> 16.4 us  [local(): pl.pallas_call(functools.partial(kernel, n, parts, layers, rank, tokens,...]
where the time goes in v2:
time: 18.4 us; the launch traced here: 18.3 us
  Pallas kernels  16.4 us (89%)
  local copies, waits for them, and re-layouts  1.19 us (6%)
  between operations  0.66 us (4%)
    pallas_call x1, Pallas kernels, local(): pl.pallas_call(functools.partial(kernel, n, parts, layers, rank, tokens,...  16.4 us
    unnamed x1, local copies, waits for them, and re-layouts  1.19 us

profile of v2, /device:TPU:0, one launch (start us, length us, event | category | flops | bytes accessed | tf_op | source)
XLA Modules:
  0.0 18.3 jit_solution(6869617363749606655)
XLA Ops:
  0.7 16.4 %shard_map.73 = f32[1,128]{1,0:T(1,128)} custom-call(s32[1]{0:T(128)S(6)} %copy.9.len_hbm, s32[16]{0:T(128)} %own_hbm.1, bf16[8,8192]{1,0:T(8,128)(2,1)} %grads_hbm.1, bf16[1,128,512]{2,1,0:T(8,128)(2,1)} %fact_hbm.1, bf16[8,32,32]{2,1,0:T(8,128)(2,1)} %bin_hbm.1, bf16[8,32,32]{2,1,0:T(8,128)(2,1)} %bout_hbm.1, f32[8,32,32]{2,1,0:T(8,128)} %eig_hbm.1), custom_call_target="tpu_custom_call" | custom-call | tf_op jit(solution)/shard_map/pallas_call | solution.py:192
  17.1 1.2 %copy.10 = f32[1,128]{1,0:T(1,128)} copy(f32[1,128]{1,0:T(1,128)} %shard_map.73) | data formatting | bytes 1024

commit v3 on v2

--- a/solution.py
+++ b/solution.py
@@ -70,17 +70,6 @@
                             device_id_type=pl.DeviceIdType.MESH)
 
     each(n - 1, greet)
-    pl.semaphore_wait(barrier, n - 1)
-
-    def send_grads(step):
-        other = (part + step + 1) % parts
-        pltpu.make_async_remote_copy(
-            grads_hbm.at[:, pl.ds(pl.multiple_of(other * share, share), share)],
-            gbuf.at[part], gsend_sem, grecv_sem,
-            device_id={"dp": group * parts + other},
-            device_id_type=pl.DeviceIdType.MESH).start()
-
-    each(parts - 1, send_grads)
 
     for load in loads[:3]:
         load.wait()
@@ -124,6 +113,8 @@
         total = jnp.where(slot == low, back[low * rows:(low + 1) * rows], total)
     hsend[...] = total.reshape(parts, chunks, LANES).astype(jnp.bfloat16)
 
+    pl.semaphore_wait(barrier, n - 1)
+
     def send_rows(step):
         peer = (me + step + 1) % n
         pltpu.make_async_remote_copy(
@@ -133,6 +124,16 @@
 
     each(n - 1, send_rows)
     hbuf[me] = hsend[part]
+
+    def send_grads(step):
+        other = (part + step + 1) % parts
+        pltpu.make_async_remote_copy(
+            grads_hbm.at[:, pl.ds(pl.multiple_of(other * share, share), share)],
+            gbuf.at[part], gsend_sem, grecv_sem,
+            device_id={"dp": group * parts + other},
+            device_id_type=pl.DeviceIdType.MESH).start()
+
+    each(parts - 1, send_grads)
 
     own_grads.wait()
     some = gbuf.at[pl.ds(0, parts - 1)]
@@ -212,7 +213,7 @@
             dma((6,)), dma, dma, dma, dma, dma, dma, dma,
         ],
         compiler_params=pltpu.CompilerParams(
-            collective_id=0, has_side_effects=True),
+            collective_id=0, has_side_effects=True, vmem_limit_bytes=55226 * 1024),
     )(lengths, owner, query_grads, train_factors, basis_in, basis_out, eigenvalues)
 
 

time: 18.4 us -> 16 us (0.87)
  Pallas kernels: 16.4 us -> 14.6 us
  local copies, waits for them, and re-layouts: 1.19 us -> 0.51 us
    pallas_call x1, Pallas kernels: 16.4 us -> 14.6 us  [local(): pl.pallas_call(functools.partial(kernel, n, parts, layers, rank, tokens,...]
    unnamed x1, local copies, waits for them, and re-layouts: 1.19 us -> 0.51 us
where the time goes in v3:
time: 16 us; the launch traced here: 15.8 us
  Pallas kernels  14.6 us (91%)
  between operations  0.66 us (4%)
  local copies, waits for them, and re-layouts  0.51 us (3%)
    pallas_call x1, Pallas kernels, local(): pl.pallas_call(functools.partial(kernel, n, parts, layers, rank, tokens,...  14.6 us
    unnamed x1, local copies, waits for them, and re-layouts  0.51 us

profile of v3, /device:TPU:0, one launch (start us, length us, event | category | flops | bytes accessed | tf_op | source)
XLA Modules:
  0.0 15.8 jit_solution(13271304961604713608)
XLA Ops:
  0.7 14.6 %shard_map.73 = f32[1,128]{1,0:T(1,128)S(1)} custom-call(s32[1]{0:T(128)S(6)} %copy.9.len_hbm, s32[16]{0:T(128)} %own_hbm.1, bf16[8,8192]{1,0:T(8,128)(2,1)} %grads_hbm.1, bf16[1,128,512]{2,1,0:T(8,128)(2,1)} %fact_hbm.1, bf16[8,32,32]{2,1,0:T(8,128)(2,1)} %bin_hbm.1, bf16[8,32,32]{2,1,0:T(8,128)(2,1)} %bout_hbm.1, f32[8,32,32]{2,1,0:T(8,128)} %eig_hbm.1), custom_call_target="tpu_custom_call" | custom-call | tf_op jit(solution)/shard_map/pallas_call | solution.py:193
  15.3 0.5 %copy.10 = f32[1,128]{1,0:T(1,128)} copy(f32[1,128]{1,0:T(1,128)S(1)} %shard_map.73) | data formatting | bytes 1024

commit v4 on v3

--- a/solution.py
+++ b/solution.py
@@ -36,12 +36,20 @@
 def kernel(n, parts, layers, rank, tokens, q_dev,
            len_hbm, own_hbm, grads_hbm, fact_hbm, bin_hbm, bout_hbm, eig_hbm,
            out_ref,
-           len_ref, own_ref, fact, b_in, b_out, eig, bo32, gbuf, hsend, hbuf, wide, score, ssend, sbuf,
+           mine, len_ref, own_ref, fact, b_in, b_out, eig, bo32, gbuf, hsend, hbuf, wide, score, ssend, sbuf,
            load_sem, gself_sem, gsend_sem, grecv_sem,
            hsend_sem, hrecv_sem, ssend_sem, srecv_sem):
     me = lax.axis_index("dp")
-    group = me // parts
+    size = 2 * parts
+    block, spot = me // size, me % size
     part = me % parts
+    hubs = n // 2
+    is_hub = spot // parts == (block + 1) % 2
+
+    def hub_at(which):
+        low = which // parts
+        return low * size + ((low + 1) % 2) * parts + which % parts
+
     width = layers * rank
     feats = layers * rank * rank
     share = feats // parts
@@ -52,24 +60,24 @@
         pltpu.make_async_copy(src, dst, load_sem.at[i])
         for i, (src, dst) in enumerate(
             [(bin_hbm, b_in), (bout_hbm, b_out), (eig_hbm, eig), (fact_hbm, fact),
-             (len_hbm, len_ref), (own_hbm, own_ref)]
+             (len_hbm, len_ref), (own_hbm, own_ref), (grads_hbm, mine)]
         )
     ]
     for load in loads:
         load.start()
-    own_grads = pltpu.make_async_copy(
-        grads_hbm.at[:, pl.ds(pl.multiple_of(part * share, share), share)],
-        gbuf.at[part], gself_sem)
-    own_grads.start()
-
     barrier = pltpu.get_barrier_semaphore()
 
-    def greet(step):
-        peer = (me + step + 1) % n
+    def signal(peer):
         pl.semaphore_signal(barrier, inc=1, device_id={"dp": peer},
                             device_id_type=pl.DeviceIdType.MESH)
 
-    each(n - 1, greet)
+    @pl.when(is_hub)
+    def _():
+        each(n - 1, lambda step: signal((me + step + 1) % n))
+
+    @pl.when(jnp.logical_not(is_hub))
+    def _():
+        each(hubs, lambda step: signal(hub_at(step)))
 
     for load in loads[:3]:
         load.wait()
@@ -113,70 +121,98 @@
         total = jnp.where(slot == low, back[low * rows:(low + 1) * rows], total)
     hsend[...] = total.reshape(parts, chunks, LANES).astype(jnp.bfloat16)
 
-    pl.semaphore_wait(barrier, n - 1)
+    @pl.when(is_hub)
+    def _():
+        pl.semaphore_wait(barrier, n - 1)
+
+    @pl.when(jnp.logical_not(is_hub))
+    def _():
+        pl.semaphore_wait(barrier, hubs)
 
     def send_rows(step):
-        peer = (me + step + 1) % n
-        pltpu.make_async_remote_copy(
-            hsend.at[peer % parts], hbuf.at[me],
-            hsend_sem, hrecv_sem, device_id={"dp": peer},
-            device_id_type=pl.DeviceIdType.MESH).start()
-
-    each(n - 1, send_rows)
-    hbuf[me] = hsend[part]
-
-    def send_grads(step):
-        other = (part + step + 1) % parts
-        pltpu.make_async_remote_copy(
-            grads_hbm.at[:, pl.ds(pl.multiple_of(other * share, share), share)],
-            gbuf.at[part], gsend_sem, grecv_sem,
-            device_id={"dp": group * parts + other},
-            device_id_type=pl.DeviceIdType.MESH).start()
-
-    each(parts - 1, send_grads)
-
-    own_grads.wait()
-    some = gbuf.at[pl.ds(0, parts - 1)]
-    pltpu.make_async_copy(some, some, grecv_sem).wait()
-    grads = gbuf[...].astype(jnp.float32).reshape(parts * q_dev, share).astype(jnp.bfloat16)
-    grads = jnp.concatenate([grads] * (LANES // (parts * q_dev)), axis=0)
-    others = hbuf.at[pl.ds(0, n - 1)]
-    pltpu.make_async_copy(others, others, hrecv_sem).wait()
-    wide[...] = hbuf[...].astype(jnp.float32).reshape(n * chunks, LANES)
-    sums = jnp.concatenate(
-        [wide[pl.ds(c, n, stride=chunks), :].astype(jnp.bfloat16) for c in range(chunks)], axis=1)
-    score[...] = nt_dot(sums, grads)
-
-    def order(step):
-        ssend[step] = score[pl.ds(own_ref[step], 1), :]
-
-    each(n, order)
-
-    def send_score(step):
-        peer = (me + step + 1) % n
-        pltpu.make_async_remote_copy(
-            ssend.at[peer], sbuf.at[me], ssend_sem, srecv_sem, device_id={"dp": peer},
-            device_id_type=pl.DeviceIdType.MESH).start()
-
-    each(n - 1, send_score)
-    sbuf[me] = ssend[me]
-    rest = sbuf.at[pl.ds(0, n - 1)]
-    pltpu.make_async_copy(rest, rest, srecv_sem).wait()
+        peer = hub_at(step)
+
+        @pl.when(peer != me)
+        def _():
+            pltpu.make_async_remote_copy(
+                hsend.at[step % parts], hbuf.at[me],
+                hsend_sem, hrecv_sem, device_id={"dp": peer},
+                device_id_type=pl.DeviceIdType.MESH).start()
+
+    each(hubs, send_rows)
+
+    def share_of(which):
+        return mine.at[:, pl.ds(which * share, share)]
+
+    for step in range(parts):
+        peer = hub_at(block * parts + step)
+
+        @pl.when(peer != me)
+        def _():
+            pltpu.make_async_remote_copy(
+                share_of(step), gbuf.at[spot], gsend_sem, grecv_sem,
+                device_id={"dp": peer}, device_id_type=pl.DeviceIdType.MESH).start()
+
+        @pl.when(peer == me)
+        def _():
+            pltpu.make_async_copy(share_of(step), gbuf.at[spot], gself_sem).start()
+
+    def take(ref, count, sem):
+        some = ref.at[pl.ds(0, count)]
+        pltpu.make_async_copy(some, some, sem).wait()
+
+    @pl.when(is_hub)
+    def _():
+        hbuf[me] = hsend[part]
+        pltpu.make_async_copy(share_of(0), gbuf.at[spot], gself_sem).wait()
+        take(gbuf, size - 1, grecv_sem)
+        grads = gbuf[...].astype(jnp.float32).reshape(size * q_dev, share).astype(jnp.bfloat16)
+        grads = jnp.concatenate([grads] * (LANES // (size * q_dev)), axis=0)
+        take(hbuf, n - 1, hrecv_sem)
+        wide[...] = hbuf[...].astype(jnp.float32).reshape(n * chunks, LANES)
+        sums = jnp.concatenate(
+            [wide[pl.ds(c, n, stride=chunks), :].astype(jnp.bfloat16) for c in range(chunks)],
+            axis=1)
+        score[...] = nt_dot(sums, grads)
+
+        slot_of_me = block * parts + part
+
+        def send_score(step):
+            peer = (me + step + 1) % n
+            ssend[peer] = score[pl.ds(own_ref[peer], 1), :]
+            pltpu.make_async_remote_copy(
+                ssend.at[peer], sbuf.at[slot_of_me], ssend_sem, srecv_sem,
+                device_id={"dp": peer}, device_id_type=pl.DeviceIdType.MESH).start()
+
+        each(n - 1, send_score)
+        sbuf[slot_of_me] = score[pl.ds(own_ref[me], 1), :]
+        take(sbuf, hubs - 1, srecv_sem)
+
+    @pl.when(jnp.logical_not(is_hub))
+    def _():
+        take(sbuf, hubs, srecv_sem)
 
     scale = 1.0 / (rank * math.sqrt(tokens))
-    span = parts * q_dev
+    span = size * q_dev
     lane = iota((1, LANES), 1) // span
     per_block = LANES // span
-    for block in range(n // parts // per_block):
+    for tile in range(n // size // per_block):
         row = jnp.zeros((1, LANES), jnp.float32)
         for at in range(per_block):
-            low = (block * per_block + at) * parts
+            low = (tile * per_block + at) * parts
             row = jnp.where(lane == at, jnp.sum(sbuf[low:low + parts], axis=0), row)
-        out_ref[:, block * LANES:(block + 1) * LANES] = row * scale
-
-    pltpu.make_async_copy(some, some, gsend_sem).wait()
-    pltpu.make_async_copy(others, others, hsend_sem).wait()
-    pltpu.make_async_copy(rest, rest, ssend_sem).wait()
+        out_ref[:, tile * LANES:(tile + 1) * LANES] = row * scale
+
+    @pl.when(is_hub)
+    def _():
+        take(gbuf, parts - 1, gsend_sem)
+        take(hbuf, hubs - 1, hsend_sem)
+        take(ssend, n - 1, ssend_sem)
+
+    @pl.when(jnp.logical_not(is_hub))
+    def _():
+        take(gbuf, parts, gsend_sem)
+        take(hbuf, hubs, hsend_sem)
 
 
 def local(query_grads, train_factors, lengths, owner, basis_in, basis_out, eigenvalues):
@@ -184,7 +220,7 @@
     n = lax.axis_size("dp")
     seqs, tokens, cols = train_factors.shape
     q_dev, feats = query_grads.shape
-    parts = feats // (SUB * LANES)
+    parts = feats // (2 * SUB * LANES)
     share = feats // parts
     width = layers * rank
     chunks = share // LANES
@@ -196,6 +232,7 @@
         in_specs=[hbm] * 7,
         out_specs=pl.BlockSpec(memory_space=pltpu.VMEM),
         scratch_shapes=[
+            pltpu.VMEM(query_grads.shape, jnp.bfloat16),
             pltpu.SMEM(lengths.shape, jnp.int32),
             pltpu.SMEM(owner.shape, jnp.int32),
             pltpu.VMEM((seqs, tokens, cols), jnp.bfloat16),
@@ -203,14 +240,14 @@
             pltpu.VMEM((layers, rank, rank), jnp.bfloat16),
             pltpu.VMEM((layers, rank, rank), jnp.float32),
             pltpu.VMEM((width, rank), jnp.float32),
-            pltpu.VMEM((parts, q_dev, share), jnp.bfloat16),
+            pltpu.VMEM((2 * parts, q_dev, share), jnp.bfloat16),
             pltpu.VMEM((parts, chunks, LANES), jnp.bfloat16),
             pltpu.VMEM((n, chunks, LANES), jnp.bfloat16),
             pltpu.VMEM((n * chunks, LANES), jnp.float32),
             pltpu.VMEM((n, LANES), jnp.float32),
             pltpu.VMEM((n, 1, LANES), jnp.float32),
-            pltpu.VMEM((n, 1, LANES), jnp.float32),
-            dma((6,)), dma, dma, dma, dma, dma, dma, dma,
+            pltpu.VMEM((n // 2, 1, LANES), jnp.float32),
+            dma((7,)), dma, dma, dma, dma, dma, dma, dma,
         ],
         compiler_params=pltpu.CompilerParams(
             collective_id=0, has_side_effects=True, vmem_limit_bytes=55226 * 1024),

time: 16 us -> 16 us (level)
  no operation moved by 1% of the time
where the time goes in v4:
time: 16 us; the launch traced here: 15.8 us
  Pallas kernels  14.6 us (91%)
  between operations  0.66 us (4%)
  local copies, waits for them, and re-layouts  0.51 us (3%)
    pallas_call x1, Pallas kernels, local(): pl.pallas_call(functools.partial(kernel, n, parts, layers, rank, tokens,...  14.6 us
    unnamed x1, local copies, waits for them, and re-layouts  0.51 us

profile of v4, /device:TPU:0, one launch (start us, length us, event | category | flops | bytes accessed | tf_op | source)
XLA Modules:
  0.0 15.8 jit_solution(13288513938358127870)
XLA Ops:
  0.7 14.6 %shard_map.73 = f32[1,128]{1,0:T(1,128)S(1)} custom-call(s32[1]{0:T(128)S(6)} %copy.9.len_hbm, s32[16]{0:T(128)} %own_hbm.1, bf16[8,8192]{1,0:T(8,128)(2,1)} %grads_hbm.1, bf16[1,128,512]{2,1,0:T(8,128)(2,1)} %fact_hbm.1, bf16[8,32,32]{2,1,0:T(8,128)(2,1)} %bin_hbm.1, bf16[8,32,32]{2,1,0:T(8,128)(2,1)} %bout_hbm.1, f32[8,32,32]{2,1,0:T(8,128)} %eig_hbm.1), custom_call_target="tpu_custom_call" | custom-call | tf_op jit(solution)/shard_map/pallas_call | solution.py:229
  15.3 0.5 %copy.10 = f32[1,128]{1,0:T(1,128)} copy(f32[1,128]{1,0:T(1,128)S(1)} %shard_map.73) | data formatting | bytes 1024

commit v5 on v3

--- a/solution.py
+++ b/solution.py
@@ -147,18 +147,15 @@
         [wide[pl.ds(c, n, stride=chunks), :].astype(jnp.bfloat16) for c in range(chunks)], axis=1)
     score[...] = nt_dot(sums, grads)
 
-    def order(step):
-        ssend[step] = score[pl.ds(own_ref[step], 1), :]
-
-    each(n, order)
-
     def send_score(step):
         peer = (me + step + 1) % n
+        ssend[peer] = score[pl.ds(own_ref[peer], 1), :]
         pltpu.make_async_remote_copy(
             ssend.at[peer], sbuf.at[me], ssend_sem, srecv_sem, device_id={"dp": peer},
             device_id_type=pl.DeviceIdType.MESH).start()
 
     each(n - 1, send_score)
+    ssend[me] = score[pl.ds(own_ref[me], 1), :]
     sbuf[me] = ssend[me]
     rest = sbuf.at[pl.ds(0, n - 1)]
     pltpu.make_async_copy(rest, rest, srecv_sem).wait()

time: 16 us -> 15.9 us (level)
  no operation moved by 1% of the time
where the time goes in v5:
time: 15.9 us; the launch traced here: 15.8 us
  Pallas kernels  14.6 us (92%)
  between operations  0.66 us (4%)
  local copies, waits for them, and re-layouts  0.51 us (3%)
    pallas_call x1, Pallas kernels, local(): pl.pallas_call(functools.partial(kernel, n, parts, layers, rank, tokens,...  14.6 us
    unnamed x1, local copies, waits for them, and re-layouts  0.51 us

profile of v5, /device:TPU:0, one launch (start us, length us, event | category | flops | bytes accessed | tf_op | source)
XLA Modules:
  0.0 15.8 jit_solution(16777777513066690410)
XLA Ops:
  0.7 14.6 %shard_map.73 = f32[1,128]{1,0:T(1,128)S(1)} custom-call(s32[1]{0:T(128)S(6)} %copy.9.len_hbm, s32[16]{0:T(128)} %own_hbm.1, bf16[8,8192]{1,0:T(8,128)(2,1)} %grads_hbm.1, bf16[1,128,512]{2,1,0:T(8,128)(2,1)} %fact_hbm.1, bf16[8,32,32]{2,1,0:T(8,128)(2,1)} %bin_hbm.1, bf16[8,32,32]{2,1,0:T(8,128)(2,1)} %bout_hbm.1, f32[8,32,32]{2,1,0:T(8,128)} %eig_hbm.1), custom_call_target="tpu_custom_call" | custom-call | tf_op jit(solution)/shard_map/pallas_call | solution.py:190
  15.3 0.5 %copy.10 = f32[1,128]{1,0:T(1,128)} copy(f32[1,128]{1,0:T(1,128)S(1)} %shard_map.73) | data formatting | bytes 1024
